TPU v7x, 32 devices: a whole 2x2x4 slice. The times are simulated.
32 devices in a mesh: groups: 2 (over x), gx: 8 (over z, y), gy: 2 (over core).
Axes of the slice: x: 2, y: 2, z: 4, core: 2. Of those that a mesh axis runs over, the one named last changes fastest.
Arguments:
- currents: bfloat16 [64, 8, 2, 128, 256], P(('groups', 'gx'), 'gy'), parts along dimension 0, may hold values from -6 to 6
- self_blocks: bfloat16 [64, 8, 2, 256, 256], P(('groups', 'gx'), 'gy'), parts along dimension 0, may hold values from -0.25 to 0.25
- near_blocks: bfloat16 [16, 2, 40, 2, 256, 256], P(('groups', 'gx'), 'gy'), parts along dimension 0, may hold values from -0.25 to 0.25
- near_pairs: int32 [16, 2, 40, 2], P(('groups', 'gx'), 'gy'), parts along dimension 0, may hold values from 0 to 15, as said below
- near_count: int32 [16, 2], P(('groups', 'gx'), 'gy'), parts along dimension 0, may hold values from 1 to 40, as said below
- basis: bfloat16 [64, 8, 2, 32, 256], P(('groups', 'gx'), 'gy'), parts along dimension 0, may hold values from -0.375 to 0.375
- transfer: bfloat16 [64, 8, 2, 1024], P(('groups', 'gx'), 'gy'), parts along dimension 0, may hold values from -0.75 to 0.75
- coupling: bfloat16 [128, 64, 2, 1024], P(('groups', 'gx', 'gy')), parts along dimension 0, may hold values from -0.09375 to 0.09375
- far_shift: int32 [128, 64, 2], P(('groups', 'gx', 'gy')), parts along dimension 0, may hold values from -1 to 1
- far_mask: int32 [128, 64], P(('groups', 'gx', 'gy')), parts along dimension 0, may hold values 0 or 1
- parent: int32 [64, 8], P(('groups', 'gx'), 'gy'), parts along dimension 0, may hold values from 0 to 63, as said below
- bloch: float32 [4], P('groups'), parts along dimension 0, may hold values from -3.140625 to 3.140625
Outputs:
- product: bfloat16 [64, 8, 2, 128, 256], P(('groups', 'gx'), 'gy'), parts along dimension 0
There are 2 independent parts, one for each index of `groups`. A program takes and returns all parts, laid end to end along the dimension named above; each array names one. Nothing has to cross between parts.
Inputs may be any that keep to these rules, and one draw needn't show every extreme that they name: `near_pairs`: column 0 is a block of the tile numbered i * 4 + j, column 1 a neighbour direction from 0 to 7; slots at or past the tile's live count hold entries of the same law. `near_count`: some tile holds exactly 40 live slots. A block of tile (tx, ty) has its parent among the 4 clusters from 4 * (tx * 2 + ty) on.
All inputs are finite; a program needn't handle non-finite values. No bound on the sum of `far_mask` on one device may be relied on, other than what follows from the above.
Results may differ from a plain program's by a relative error of at most 0.0042.
Values may be sent and summed in bfloat16 or wider, within the bound.
No kernel may reach another device: no remote copies, remote signals or barrier semaphores. Data moves between devices by JAX's collectives and lax.ppermute only.
A program may use at most 192 MiB of HBM per device.

v0:
```python
import jax
import jax.numpy as jnp
from jax import lax
from jax.sharding import PartitionSpec as P

HIGH = lax.Precision.HIGHEST


def extended_2(cells, sides, width):
    for axis, dim in sides:
        count = lax.axis_size(axis)
        head = lax.slice_in_dim(cells, 0, width, axis=dim)
        tail = lax.slice_in_dim(cells, cells.shape[dim] - width, cells.shape[dim], axis=dim)
        cells = jnp.concatenate(
            [
                lax.ppermute(tail, axis, [(i, (i + 1) % count) for i in range(count)]),
                cells,
                lax.ppermute(head, axis, [((i + 1) % count, i) for i in range(count)]),
            ],
            axis=dim,
        )
    return cells


def combine_planes(raw, half):
    real = raw[:, 0, :half] - raw[:, 1, half:]
    imag = raw[:, 0, half:] + raw[:, 1, :half]
    return jnp.concatenate([real, imag], axis=1)


def per_device(
    currents,
    self_blocks,
    near_blocks,
    near_pairs,
    near_count,
    basis,
    transfer,
    coupling,
    far_shift,
    far_mask,
    parent,
    bloch,
):
    tile_x, tile_y, _, rhs_count, panels = currents.shape
    rank = basis.shape[3]
    blocks = tile_x * tile_y
    wide_x = tile_x + 2
    wide_y = tile_y + 2
    gx_count = lax.axis_size("gx")
    gy_count = lax.axis_size("gy")
    gx_index = lax.axis_index("gx")
    gy_index = lax.axis_index("gy")
    extended = extended_2(currents, (("gx", 0), ("gy", 1)), 1)
    window = extended.reshape(wide_x * wide_y, 2 * rhs_count, panels)
    pair_table = near_pairs.reshape(-1, 2)
    slots = pair_table.shape[0]
    row_local = pair_table[:, 0]
    direction = pair_table[:, 1]
    offset = direction + (direction >= 4).astype(jnp.int32)
    row_x = row_local // tile_y
    row_y = row_local % tile_y
    col_x = row_x + offset // 3
    col_y = row_y + offset % 3
    row_cell = (row_x + 1) * wide_y + row_y + 1
    col_cell = col_x * wide_y + col_y
    shift_x = jnp.where((col_x == wide_x - 1) & (gx_index == gx_count - 1), 1.0, 0.0) - jnp.where(
        (col_x == 0) & (gx_index == 0), 1.0, 0.0
    )
    shift_y = jnp.where((col_y == wide_y - 1) & (gy_index == gy_count - 1), 1.0, 0.0) - jnp.where(
        (col_y == 0) & (gy_index == 0), 1.0, 0.0
    )
    phases = bloch[0] * shift_x + bloch[1] * shift_y
    phase_cos = jnp.cos(phases)[:, None, None]
    phase_sin = jnp.sin(phases)[:, None, None]
    alive_mask = (jnp.arange(slots) < near_count.reshape(())).astype(jnp.float32)
    near_mats = near_blocks.reshape(slots, 2, panels, panels)
    cells = wide_x * wide_y
    sources = jnp.take(window, col_cell, axis=0).astype(jnp.float32)
    row_vals = jnp.take(window, row_cell, axis=0).astype(jnp.float32)
    src_re = sources[:, :rhs_count]
    src_im = sources[:, rhs_count:]
    row_re = row_vals[:, :rhs_count]
    row_im = row_vals[:, rhs_count:]
    column_source = jnp.concatenate(
        [phase_cos * src_re - phase_sin * src_im, phase_sin * src_re + phase_cos * src_im], axis=1
    ).astype(jnp.bfloat16)
    row_source = jnp.concatenate(
        [phase_cos * row_re + phase_sin * row_im, phase_cos * row_im - phase_sin * row_re], axis=1
    ).astype(jnp.bfloat16)
    forward = combine_planes(
        jnp.einsum("scpq,sjq->scjp", near_mats, column_source, preferred_element_type=jnp.float32),
        rhs_count,
    )
    transposed = combine_planes(
        jnp.einsum("scpq,sjp->scjq", near_mats, row_source, preferred_element_type=jnp.float32),
        rhs_count,
    )
    cell_ids = jnp.arange(cells)[None, :]
    row_hot = (row_cell[:, None] == cell_ids).astype(jnp.float32) * alive_mask[:, None]
    col_hot = (col_cell[:, None] == cell_ids).astype(jnp.float32) * alive_mask[:, None]
    width = forward.shape[0]
    totals = jnp.dot(row_hot.T, forward.reshape(width, -1), precision=HIGH) + jnp.dot(
        col_hot.T, transposed.reshape(width, -1), precision=HIGH
    )
    totals = totals.reshape(wide_x, wide_y, 2, rhs_count, panels)
    outer_rows = jnp.stack([totals[0], totals[wide_x - 1]], axis=0)
    rows_back = extended_2(outer_rows.astype(jnp.bfloat16), (("gx", 0),), 1).astype(
        outer_rows.dtype
    )
    totals = totals.at[1].add(rows_back[0]).at[tile_x].add(rows_back[3])
    outer_cols = jnp.stack([totals[1 : tile_x + 1, 0], totals[1 : tile_x + 1, wide_y - 1]], axis=1)
    cols_back = extended_2(outer_cols.astype(jnp.bfloat16), (("gy", 1),), 1).astype(
        outer_cols.dtype
    )
    inner = totals[1 : tile_x + 1, 1 : tile_y + 1]
    inner = inner.at[:, 0].add(cols_back[:, 0]).at[:, tile_y - 1].add(cols_back[:, 3])
    block_cur = currents.reshape(blocks, 2 * rhs_count, panels)
    self_mats = self_blocks.reshape(blocks, 2, panels, panels)
    self_field = combine_planes(
        jnp.einsum("scpq,sjq->scjp", self_mats, block_cur, preferred_element_type=jnp.float32),
        rhs_count,
    )
    basis_b = basis.reshape(blocks, 2, rank, panels)
    leaf_raw = jnp.einsum("sckp,sjp->sckj", basis_b, block_cur, preferred_element_type=jnp.float32)
    leaf_real = leaf_raw[:, 0, :, :rhs_count] - leaf_raw[:, 1, :, rhs_count:]
    leaf_imag = leaf_raw[:, 0, :, rhs_count:] + leaf_raw[:, 1, :, :rhs_count]
    transfer_f = transfer.astype(jnp.float32).reshape(blocks, 2, rank, rank)
    lift_real = jnp.einsum(
        "skl,slR->skR", transfer_f[:, 0], leaf_real, precision=HIGH
    ) - jnp.einsum("skl,slR->skR", transfer_f[:, 1], leaf_imag, precision=HIGH)
    lift_imag = jnp.einsum(
        "skl,slR->skR", transfer_f[:, 0], leaf_imag, precision=HIGH
    ) + jnp.einsum("skl,slR->skR", transfer_f[:, 1], leaf_real, precision=HIGH)
    own_clusters = far_mask.shape[0]
    cluster_base = (gx_index * gy_count + gy_index) * own_clusters
    local_parent = parent.reshape(blocks) - cluster_base
    cluster_hot = (local_parent[:, None] == jnp.arange(own_clusters)[None, :]).astype(jnp.float32)
    lifted = jnp.stack([lift_real, lift_imag], axis=1).reshape(blocks, -1)
    cluster_coeff = (
        jnp.dot(cluster_hot.T, lifted, precision=HIGH)
        .reshape(own_clusters, 2, rank, rhs_count)
        .astype(jnp.bfloat16)
    )
    shard_coeff = lax.all_gather(cluster_coeff, ("gx", "gy"), axis=0, tiled=True)
    piece_rows = shard_coeff.shape[0]
    mats = coupling.reshape(own_clusters, piece_rows, 2, rank, rank)
    prod = jnp.einsum("pqckl,qdlR->pqcdkR", mats, shard_coeff, preferred_element_type=jnp.float32)
    prod_real = prod[:, :, 0, 0] - prod[:, :, 1, 1]
    prod_imag = prod[:, :, 0, 1] + prod[:, :, 1, 0]
    shifts = far_shift.astype(jnp.float32)
    keep = far_mask.astype(jnp.float32)
    pair_phase = bloch[0] * shifts[..., 0] + bloch[1] * shifts[..., 1]
    weight_cos = (keep * jnp.cos(pair_phase))[:, :, None, None]
    weight_sin = (keep * jnp.sin(pair_phase))[:, :, None, None]
    real = jnp.sum(weight_cos * prod_real - weight_sin * prod_imag, axis=1)
    imag = jnp.sum(weight_sin * prod_real + weight_cos * prod_imag, axis=1)
    far_local = jnp.stack([real, imag], axis=1)
    chosen = jnp.dot(cluster_hot, far_local.reshape(own_clusters, -1), precision=HIGH).reshape(
        blocks, 2, rank, rhs_count
    )
    down_real = jnp.einsum(
        "skl,skR->slR", transfer_f[:, 0], chosen[:, 0], precision=HIGH
    ) - jnp.einsum("skl,skR->slR", transfer_f[:, 1], chosen[:, 1], precision=HIGH)
    down_imag = jnp.einsum(
        "skl,skR->slR", transfer_f[:, 0], chosen[:, 1], precision=HIGH
    ) + jnp.einsum("skl,skR->slR", transfer_f[:, 1], chosen[:, 0], precision=HIGH)
    down_coeff = jnp.stack([down_real, down_imag], axis=1).astype(jnp.bfloat16)
    far_raw = jnp.einsum(
        "sckp,sdkR->scdRp", basis_b, down_coeff, preferred_element_type=jnp.float32
    )
    far_field = jnp.stack(
        [far_raw[:, 0, 0] - far_raw[:, 1, 1], far_raw[:, 0, 1] + far_raw[:, 1, 0]], axis=1
    )
    local_sum = (self_field.reshape(blocks, 2, rhs_count, panels) + far_field).reshape(
        tile_x, tile_y, 2, rhs_count, panels
    )
    return (inner + local_sum).astype(jnp.bfloat16)


def solution(mesh):
    placed = (
        P(("groups", "gx"), "gy", None, None, None),
        P(("groups", "gx"), "gy", None, None, None),
        P(("groups", "gx"), "gy", None, None, None, None),
        P(("groups", "gx"), "gy", None, None),
        P(("groups", "gx"), "gy"),
        P(("groups", "gx"), "gy", None, None, None),
        P(("groups", "gx"), "gy", None, None),
        P(("groups", "gx", "gy"), None, None, None),
        P(("groups", "gx", "gy"), None, None),
        P(("groups", "gx", "gy"), None),
        P(("groups", "gx"), "gy"),
        P("groups"),
    )
    return jax.shard_map(
        per_device,
        mesh=mesh,
        in_specs=placed,
        out_specs=P(("groups", "gx"), "gy", None, None, None),
        check_vma=False,
    )
```

profile of v0, /device:TPU:0, one launch (start us, length us, event | category | flops | bytes accessed | tf_op | source)
XLA Modules:
  0.0 295.7 jit_solution(5326752503115041314)
XLA Ops:
  8.9 3.0 %collective-permute-start = (bf16[1,4,2,128,256]{4,3,2,1,0:T(8,128)(2,1)}, bf16[1,4,2,128,256]{4,3,2,1,0:T(8,128)(2,1)}, u32[]{:S(2)}, u32[]{:S(2)}) collective-permute-start(bf16[1,4,2,128,256]{4,3,2,1,0:T(8,128)(2,1)} %get-tuple-element.82), channel_id=1, source_target_pairs={{0,2},{2,4},{4,6},{6,8},{8,10},{10,12},{12,14},{14,0},{1,3},{3,5},... | collective-permute-start | bytes 1572872 | tf_op jit(solution)/shard_map/ppermute | solution.py:16
  11.9 3.0 %collective-permute-start.1 = (bf16[1,4,2,128,256]{4,3,2,1,0:T(8,128)(2,1)}, bf16[1,4,2,128,256]{4,3,2,1,0:T(8,128)(2,1)}, u32[]{:S(2)}, u32[]{:S(2)}) collective-permute-start(bf16[1,4,2,128,256]{4,3,2,1,0:T(8,128)(2,1)} %get-tuple-element.81), channel_id=1, source_target_pairs={{2,0},{4,2},{6,4},{8,6},{10,8},{12,10},{14,12},{0,14},{3,1},{5,3},... | collective-permute-start | bytes 1572872 | tf_op jit(solution)/shard_map/ppermute | solution.py:18
  24.3 3.5 %convolution_bitcast_fusion.2 = f32[16,2,256,256]{3,2,1,0:T(8,128)S(1)} fusion(bf16[16,256,256,1]{2,1,3,0:T(8,128)(2,1)S(1)} %bitcast.277, bf16[16,2,256,256]{3,2,1,0:T(8,128)(2,1)} %bitcast.290), kind=kOutput, calls=%fused_computation.50 | convolution fusion | flops 1073741824 | bytes 14680064 | tf_op jit(solution)/shard_map/scpq,sjq->scjp/dot_general | solution.py:121
  42.2 3.1 %copy.102 = bf16[4,64,2,1024]{1,3,2,0:T(8,128)(2,1)S(1)} copy(bf16[4,64,2,1024]{3,2,1,0:T(2,128)(2,1)} %param.29) | data formatting | bytes 2097152 | tf_op args[7]
  45.3 6.9 %copy.123 = bf16[4,64,2,32,32,1]{4,3,2,0,5,1:T(8,128)(2,1)} copy(bf16[4,64,2,32,32,1]{1,4,3,2,0,5:T(8,128)(2,1)S(1)} %bitcast.279) | data formatting | bytes 2097152 | tf_op jit(solution)/shard_map/reshape | solution.py:147
  52.2 4.8 %pad_maximum_fusion.3 = f32[16,256,256]{2,1,0:T(8,128)} fusion(f32[16,128,256]{2,1,0:T(8,128)} %fusion.25, f32[16,128,256]{2,1,0:T(8,128)} %fusion.27), kind=kLoop, calls=%fused_computation.43 | loop fusion | flops 1048576 | bytes 8388608 | tf_op jit(solution)/shard_map/concatenate | solution.py:28
  57.0 3.5 %pad_maximum_fusion.2 = bf16[6,6,2,128,256]{4,3,2,1,0:T(8,128)(2,1)} fusion(bf16[6,1,2,128,256]{4,3,2,1,0:T(8,128)(2,1)S(1)} %collective-permute-done.3, bf16[6,4,2,128,256]{4,3,2,1,0:T(8,128)(2,1)S(1)} %copy-done.6, bf16[6,1,2,128,256]{4,3,2,1,0:T(8,128)(2,1)} %collective-permute-done.2), kind=kLoop, calls=%fused_computation.36 | loop fusion | flops 4718592 | bytes 9437184 | tf_op jit(solution)/shard_map/concatenate | solution.py:14
  60.5 7.0 %gather_fusion.1 = bf16[40,256,256]{2,1,0:T(8,128)(2,1)} fusion(bf16[36,256,256]{2,1,0:T(8,128)(2,1)} %bitcast.270, s32[1024]{0:T(1024)S(1)} %get-tuple-element.93), kind=kCustom, calls=%fused_computation.1.clone | custom fusion | bytes 10485920 | tf_op jit(solution)/shard_map/jit(_take)/gather | solution.py:80
  67.5 7.0 %gather_fusion = bf16[40,256,256]{2,1,0:T(8,128)(2,1)} fusion(bf16[36,256,256]{2,1,0:T(8,128)(2,1)} %bitcast.271, s32[1024]{0:T(1024)S(1)} %get-tuple-element.94), kind=kCustom, calls=%fused_computation.clone | custom fusion | bytes 10485920 | tf_op jit(solution)/shard_map/jit(_take)/gather | solution.py:79
  74.5 3.2 %select_convert_fusion = f32[40,256,256]{2,1,0:T(8,128)S(1)} fusion(bf16[40,256,256]{2,1,0:T(8,128)(2,1)} %gather_fusion.1, pred[40]{0:T(512)(128)(4,1)S(1)} %get-tuple-element.59), kind=kLoop, calls=%fused_computation.30 | loop fusion | flops 5242880 | bytes 15728680 | tf_op jit(solution)/shard_map/convert_element_type | solution.py:80
  77.8 3.2 %select_convert_fusion.1 = f32[40,256,256]{2,1,0:T(8,128)S(1)} fusion(bf16[40,256,256]{2,1,0:T(8,128)(2,1)} %gather_fusion, pred[40]{0:T(512)(128)(4,1)S(1)} %get-tuple-element.67), kind=kLoop, calls=%fused_computation.31 | loop fusion | flops 5242880 | bytes 15728680 | tf_op jit(solution)/shard_map/convert_element_type | solution.py:79
  81.0 6.8 %add_convert_fusion = (bf16[40,128,256]{2,1,0:T(8,128)(2,1)}, bf16[40,128,256]{2,1,0:T(8,128)(2,1)}, bf16[40,128,256]{2,1,0:T(8,128)(2,1)}, bf16[40,128,256]{2,1,0:T(8,128)(2,1)}) fusion(f32[40,256,256]{2,1,0:T(8,128)S(1)} %select_convert_fusion, f32[40]{0:T(128)S(1)} %sin.13, f32[40]{0:T(128)S(1)} %get-tuple-element.63, ...), kind=kLoop, calls=%fused_computation.33 | loop fusion | flops 20971520 | bytes 31457600 | tf_op jit(solution)/shard_map/convert.16
  87.8 12.8 %fusion.4 = f32[40,2,256,256]{3,2,1,0:T(8,128)} fusion(bf16[1,1,40,2,256,256]{5,4,3,2,1,0:T(8,128)(2,1)} %param.24, bf16[40,128,256]{2,1,0:T(8,128)(2,1)} %get-tuple-element.87, bf16[40,128,256]{2,1,0:T(8,128)(2,1)} %get-tuple-element.88), kind=kOutput, calls=%fused_computation.9 | convolution fusion | flops 2694840320 | bytes 36700160 | tf_op jit(solution)/shard_map/scpq,sjq->scjp/dot_general | solution.py:92
  100.6 7.3 %fusion.13 = f32[40,128,256]{2,1,0:T(8,128)} fusion(f32[40,2,256,256]{3,2,1,0:T(8,128)} %fusion.4), kind=kLoop, calls=%fused_computation.19 | loop fusion | flops 1310720 | bytes 15728640 | tf_op jit(solution)/shard_map/add | solution.py:27
  108.0 7.5 %fusion.15 = f32[40,128,256]{2,1,0:T(8,128)} fusion(f32[40,2,256,256]{3,2,1,0:T(8,128)} %fusion.4), kind=kLoop, calls=%fused_computation.22 | loop fusion | flops 1310720 | bytes 15728640 | tf_op jit(solution)/shard_map/sub | solution.py:26
  115.5 14.7 %fusion.7 = f32[40,2,256,256]{3,2,1,0:T(8,128)} fusion(bf16[1,1,40,2,256,256]{5,4,3,2,1,0:T(8,128)(2,1)} %param.24, bf16[40,128,256]{2,1,0:T(8,128)(2,1)} %get-tuple-element.70, bf16[40,128,256]{2,1,0:T(8,128)(2,1)S(1)} %copy-done.4), kind=kOutput, calls=%fused_computation.10 | convolution fusion | flops 2694840320 | bytes 36700160 | tf_op jit(solution)/shard_map/scpq,sjp->scjq/dot_general | solution.py:96
  130.1 7.4 %fusion.10 = f32[40,128,256]{2,1,0:T(8,128)} fusion(f32[40,2,256,256]{3,2,1,0:T(8,128)} %fusion.7), kind=kLoop, calls=%fused_computation.13 | loop fusion | flops 1310720 | bytes 15728640 | tf_op jit(solution)/shard_map/add | solution.py:27
  137.5 7.3 %fusion.12 = f32[40,128,256]{2,1,0:T(8,128)} fusion(f32[40,2,256,256]{3,2,1,0:T(8,128)} %fusion.7), kind=kLoop, calls=%fused_computation.16 | loop fusion | flops 1310720 | bytes 15728640 | tf_op jit(solution)/shard_map/sub | solution.py:26
  144.8 9.1 %pad_maximum_fusion = f32[40,256,256]{2,1,0:T(8,128)} fusion(f32[40,128,256]{2,1,0:T(8,128)} %fusion.13, f32[40,128,256]{2,1,0:T(8,128)} %fusion.15), kind=kLoop, calls=%fused_computation.3 | loop fusion | flops 2621440 | bytes 20971520 | tf_op jit(solution)/shard_map/concatenate | solution.py:28
  153.9 14.3 %copy.142 = f32[5,8,256,256]{3,1,2,0:T(8,128)} copy(f32[5,8,256,256]{3,2,1,0:T(8,128)} %bitcast.272) | data formatting | bytes 20971520
  168.3 9.2 %pad_maximum_fusion.1 = f32[40,256,256]{2,1,0:T(8,128)} fusion(f32[40,128,256]{2,1,0:T(8,128)} %fusion.10, f32[40,128,256]{2,1,0:T(8,128)} %fusion.12), kind=kLoop, calls=%fused_computation.4 | loop fusion | flops 2621440 | bytes 20971520 | tf_op jit(solution)/shard_map/concatenate | solution.py:28
  177.5 13.9 %copy.143 = f32[5,8,256,256]{3,1,2,0:T(8,128)} copy(f32[5,8,256,256]{3,2,1,0:T(8,128)} %bitcast.273) | data formatting | bytes 20971520
  191.4 11.9 %fusion.56 = f32[36,65536]{1,0:T(8,128)} fusion(f32[40,65536]{1,0:T(8,128)S(1)} %bitcast.265, f32[40]{0:T(128)S(1)} %compare_convert_fusion.2, s32[40]{0:T(128)S(1)} %add_bitcast_fusion), kind=kOutput, calls=%fused_computation.110 | convolution fusion | flops 1132464896 | bytes 19923264 | tf_op jit(solution)/shard_map/dot_general | solution.py:103
  203.3 14.9 %fusion.92 = (bf16[36,65536]{1,0:T(8,128)(2,1)}, f32[36,65536]{1,0:T(8,128)S(1)}) fusion(f32[36,65536]{1,0:T(8,128)} %fusion.56, f32[40,65536]{1,0:T(8,128)} %bitcast.274, s32[40]{0:T(128)S(1)} %get-tuple-element.56, f32[40]{0:T(128)S(1)} %compare_convert_fusion.2), kind=kOutput, calls=%fused_computation.183 | convolution fusion | flops 1137183488 | bytes 34079040 | tf_op jit(solution)/shard_map/dot_general | solution.py:103
  218.2 3.1 %fusion.87 = (bf16[6,65536]{1,0:T(8,128)(2,1)S(1)}, bf16[6,65536]{1,0:T(8,128)(2,1)}) fusion(bf16[36,65536]{1,0:T(8,128)(2,1)} %get-tuple-element.91), kind=kLoop, calls=%fused_computation.178 | loop fusion | bytes 3145728 | tf_op jit(solution)/shard_map/slice | solution.py:107
  221.4 7.2 %copy.144 = f32[5,8,256,256]{3,2,1,0:T(8,128)} copy(f32[5,8,256,256]{3,1,2,0:T(8,128)S(1)} %bitcast.269) | data formatting | bytes 20971520
  228.7 8.4 %slice.413 = f32[36,256,256]{2,1,0:T(8,128)} slice(f32[40,256,256]{2,1,0:T(8,128)} %bitcast.275), slice={[0:36], [0:256], [0:256]} | slice | bytes 18874368
  238.9 4.6 %collective-permute-start.5 = (bf16[1,6,2,128,256]{4,3,2,1,0:T(8,128)(2,1)S(1)}, bf16[1,6,2,128,256]{4,3,2,1,0:T(8,128)(2,1)}, u32[]{:S(2)}, u32[]{:S(2)}) collective-permute-start(bf16[1,6,2,128,256]{4,3,2,1,0:T(8,128)(2,1)S(1)} %bitcast.283), channel_id=1, source_target_pairs={{2,0},{4,2},{6,4},{8,6},{10,8},{12,10},{14,12},{0,14},{3,1},{5,3},... | collective-permute-start | bytes 2359304 | tf_op jit(solution)/shard_map/ppermute | solution.py:18
  243.7 10.7 %convolution_bitcast_fusion = f32[4,64,2,2,32,128]{5,4,2,0,3,1:T(8,128)} fusion(bf16[4,64,2,32,32,1]{4,3,2,0,5,1:T(8,128)(2,1)} %copy.123, bf16[64,2,32,128]{3,2,1,0:T(8,128)(2,1)} %all-gather.2.cloned.1.call-done), kind=kOutput, calls=%fused_computation.11 | convolution fusion | flops 268435456 | bytes 18874368 | tf_op jit(solution)/shard_map/pqckl,qdlR->pqcdkR/dot_general | solution.py:148
  254.4 7.0 %subtract_reduce_fusion = (f32[4,32,128]{2,1,0:T(8,128)S(1)}, f32[4,32,128]{2,1,0:T(8,128)S(1)}) fusion(f32[4,64]{0,1:T(8,128)S(1)} %copy.106, f32[4,64]{0,1:T(8,128)S(1)} %copy.97, f32[4,64,2,2,32,128]{5,4,2,0,3,1:T(8,128)} %convolution_bitcast_fusion), kind=kLoop, calls=%fused_computation.48 | loop fusion | flops 10452992 | bytes 16910336 | tf_op jit(solution)/shard_map/reduce_sum | solution.py:156
  263.5 11.8 %collective-permute-done.5 = bf16[1,6,2,128,256]{4,3,2,1,0:T(8,128)(2,1)} collective-permute-done((bf16[1,6,2,128,256]{4,3,2,1,0:T(8,128)(2,1)S(1)}, bf16[1,6,2,128,256]{4,3,2,1,0:T(8,128)(2,1)}, u32[]{:S(2)}, u32[]{:S(2)}) %collective-permute-start.5) | collective-permute-done | bytes 786464 | tf_op jit(solution)/shard_map/ppermute | solution.py:18
  284.4 4.1 %fusion.24 = bf16[4,4,2,128,256]{4,3,2,1,0:T(8,128)(2,1)} fusion(f32[4,4,2,128,256]{4,3,2,1,0:T(8,128)S(1)} %fusion.36, f32[4,4,2,128,256]{4,3,2,1,0:T(8,128)S(1)} %bitcast.278, f32[4,4,1,128,256]{4,3,2,1,0:T(8,128)} %bitcast.282, f32[4,4,1,128,256]{4,3,2,1,0:T(8,128)S(1)} %bitcast.281), kind=kLoop, calls=%fused_computation.46 | loop fusion | flops 4194304 | bytes 14680064 | tf_op jit(solution)/shard_map/convert_element_type | solution.py:178
  (116 shorter events, 38.6 us)
Async XLA Ops:
  6.5 9.5 %copy-start = (bf16[4,4,2,32,256]{4,3,2,1,0:T(8,128)(2,1)S(1)}, bf16[4,4,2,32,256]{4,3,2,1,0:T(8,128)(2,1)}, u32[]{:S(2)}) copy-start(bf16[4,4,2,32,256]{4,3,2,1,0:T(8,128)(2,1)} %param.27) | copy-start | bytes 1572868
  6.5 237.2 %all-gather.2.cloned.1.call-start = ((), (), s32[]{:S(2)}) async-start(), calls=%async_computation | async-start | bytes 1114112 | tf_op jit(solution)/shard_map/all_gather | solution.py:145
  8.9 26.4 %collective-permute-start = (bf16[1,4,2,128,256]{4,3,2,1,0:T(8,128)(2,1)}, bf16[1,4,2,128,256]{4,3,2,1,0:T(8,128)(2,1)}, u32[]{:S(2)}, u32[]{:S(2)}) collective-permute-start(bf16[1,4,2,128,256]{4,3,2,1,0:T(8,128)(2,1)} %get-tuple-element.82), channel_id=1, source_target_pairs={{0,2},{2,4},{4,6},{6,8},{8,10},{10,12},{12,14},{14,0},{1,3},{3,5},... | collective-permute-start | bytes 1572872 | tf_op jit(solution)/shard_map/ppermute | solution.py:16
  11.9 25.6 %collective-permute-start.1 = (bf16[1,4,2,128,256]{4,3,2,1,0:T(8,128)(2,1)}, bf16[1,4,2,128,256]{4,3,2,1,0:T(8,128)(2,1)}, u32[]{:S(2)}, u32[]{:S(2)}) collective-permute-start(bf16[1,4,2,128,256]{4,3,2,1,0:T(8,128)(2,1)} %get-tuple-element.81), channel_id=1, source_target_pairs={{2,0},{4,2},{6,4},{8,6},{10,8},{12,10},{14,12},{0,14},{3,1},{5,3},... | collective-permute-start | bytes 1572872 | tf_op jit(solution)/shard_map/ppermute | solution.py:18
  16.0 6.8 %copy-start.7 = (bf16[16,2,32,32]{3,2,0,1:T(8,128)(2,1)}, bf16[16,2,32,32]{3,2,0,1:T(8,128)(2,1)S(1)}, u32[]{:S(2)}) copy-start(bf16[16,2,32,32]{3,2,0,1:T(8,128)(2,1)S(1)} %reshape.412) | copy-start | bytes 196612
  16.0 6.9 %copy-start.16 = (s32[4,4]{1,0:T(4,128)S(1)}, s32[4,4]{1,0:T(4,128)}, u32[]{:S(2)}) copy-start(s32[4,4]{1,0:T(4,128)} %param.32) | copy-start | bytes 196
  18.5 1.0 copy-start.10
  18.5 5.8 %copy-start.2 = (bf16[4,4,2,128,256]{4,3,2,1,0:T(8,128)(2,1)S(1)}, bf16[4,4,2,128,256]{4,3,2,1,0:T(8,128)(2,1)}, u32[]{:S(2)}) copy-start(bf16[4,4,2,128,256]{4,3,2,1,0:T(8,128)(2,1)} %param.22) | copy-start | bytes 6291460
  23.0 4.8 %copy-start.12 = (s32[16]{0:T(128)}, s32[16]{0:T(128)S(1)}, u32[]{:S(2)}) copy-start(s32[16]{0:T(128)S(1)} %sub.128) | copy-start | bytes 196
  29.4 1.6 copy-start.15
  29.4 1.7 copy-start.17
  29.4 2.3 copy-start.14
  29.4 4.3 %copy-start.18 = (s32[4,64]{1,0:T(4,128)S(1)}, s32[4,64]{1,0:T(4,128)}, u32[]{:S(2)}) copy-start(s32[4,64]{1,0:T(4,128)} %param.31) | copy-start | bytes 3076
  38.6 1.6 copy-start.5
  41.5 15.5 %collective-permute-start.3 = (bf16[6,1,2,128,256]{4,3,2,1,0:T(8,128)(2,1)}, bf16[6,1,2,128,256]{4,3,2,1,0:T(8,128)(2,1)S(1)}, u32[]{:S(2)}, u32[]{:S(2)}) collective-permute-start(bf16[6,1,2,128,256]{4,3,2,1,0:T(8,128)(2,1)} %get-tuple-element.80), channel_id=1, source_target_pairs={{1,0},{0,1},{3,2},{2,3},{5,4},{4,5},{7,6},{6,7},{9,8},{8,9},{11,10... | collective-permute-start | bytes 2359304 | tf_op jit(solution)/shard_map/ppermute | solution.py:18
  41.5 15.5 %collective-permute-start.2 = (bf16[6,1,2,128,256]{4,3,2,1,0:T(8,128)(2,1)}, bf16[6,1,2,128,256]{4,3,2,1,0:T(8,128)(2,1)}, u32[]{:S(2)}, u32[]{:S(2)}) collective-permute-start(bf16[6,1,2,128,256]{4,3,2,1,0:T(8,128)(2,1)} %get-tuple-element.79), channel_id=1, source_target_pairs={{0,1},{1,0},{2,3},{3,2},{4,5},{5,4},{6,7},{7,6},{8,9},{9,8},{10,11... | collective-permute-start | bytes 2359304 | tf_op jit(solution)/shard_map/ppermute | solution.py:16
  52.2 4.8 %copy-start.6 = (bf16[6,4,2,128,256]{4,3,2,1,0:T(8,128)(2,1)S(1)}, bf16[6,4,2,128,256]{4,3,2,1,0:T(8,128)(2,1)}, u32[]{:S(2)}) copy-start(bf16[6,4,2,128,256]{4,3,2,1,0:T(8,128)(2,1)} %copy-done.5) | copy-start | bytes 9437188
  108.0 7.5 %copy-start.4 = (bf16[40,128,256]{2,1,0:T(8,128)(2,1)S(1)}, bf16[40,128,256]{2,1,0:T(8,128)(2,1)}, u32[]{:S(2)}) copy-start(bf16[40,128,256]{2,1,0:T(8,128)(2,1)} %get-tuple-element.69) | copy-start | bytes 7864324
  177.5 13.9 %copy-start.1 = (f32[5,8,256,256]{3,1,2,0:T(8,128)S(1)}, f32[5,8,256,256]{3,1,2,0:T(8,128)}, u32[]{:S(2)}) copy-start(f32[5,8,256,256]{3,1,2,0:T(8,128)} %copy.142) | copy-start | bytes 31457284
  228.7 10.0 %copy-start.11 = (bf16[6,65536]{1,0:T(8,128)(2,1)S(1)}, bf16[6,65536]{1,0:T(8,128)(2,1)}, u32[]{:S(2)}) copy-start(bf16[6,65536]{1,0:T(8,128)(2,1)} %get-tuple-element.76) | copy-start | bytes 2359300
  238.9 36.5 %collective-permute-start.5 = (bf16[1,6,2,128,256]{4,3,2,1,0:T(8,128)(2,1)S(1)}, bf16[1,6,2,128,256]{4,3,2,1,0:T(8,128)(2,1)}, u32[]{:S(2)}, u32[]{:S(2)}) collective-permute-start(bf16[1,6,2,128,256]{4,3,2,1,0:T(8,128)(2,1)S(1)} %bitcast.283), channel_id=1, source_target_pairs={{2,0},{4,2},{6,4},{8,6},{10,8},{12,10},{14,12},{0,14},{3,1},{5,3},... | collective-permute-start | bytes 2359304 | tf_op jit(solution)/shard_map/ppermute | solution.py:18
  243.6 31.7 %collective-permute-start.4 = (bf16[1,6,2,128,256]{4,3,2,1,0:T(8,128)(2,1)S(1)}, bf16[1,6,2,128,256]{4,3,2,1,0:T(8,128)(2,1)S(1)}, u32[]{:S(2)}, u32[]{:S(2)}) collective-permute-start(bf16[1,6,2,128,256]{4,3,2,1,0:T(8,128)(2,1)S(1)} %bitcast.286), channel_id=1, source_target_pairs={{0,2},{2,4},{4,6},{6,8},{8,10},{10,12},{12,14},{14,0},{1,3},{3,5},... | collective-permute-start | bytes 2359304 | tf_op jit(solution)/shard_map/ppermute | solution.py:16
  243.7 31.6 %slice-start = ((s8[9437184]{0:T(1024)(128)(4,1)}), s8[4194304]{0:T(1024)(128)(4,1)S(1)}, s32[]{:S(2)}) async-start(s8[9437184]{0:T(1024)(128)(4,1)} %bitcast.266), calls=%async_computation.1 | async-start | bytes 8388608
  243.7 31.6 %slice-start.1 = ((s8[9437184]{0:T(1024)(128)(4,1)}), s8[4194304]{0:T(1024)(128)(4,1)S(1)}, s32[]{:S(2)}) async-start(s8[9437184]{0:T(1024)(128)(4,1)} %bitcast.266), calls=%async_computation.2 | async-start | bytes 8388608
  254.4 7.2 %copy-start.13 = (s32[16]{0:T(128)S(1)}, s32[16]{0:T(128)}, u32[]{:S(2)}) copy-start(s32[16]{0:T(128)} %copy-done.12) | copy-start | bytes 196
  254.4 7.7 %copy-start.8 = (bf16[16,2,32,32]{3,2,0,1:T(8,128)(2,1)S(1)}, bf16[16,2,32,32]{3,2,0,1:T(8,128)(2,1)}, u32[]{:S(2)}) copy-start(bf16[16,2,32,32]{3,2,0,1:T(8,128)(2,1)} %copy-done.7) | copy-start | bytes 196612
  254.4 20.9 %slice-start.2 = ((s8[9437184]{0:T(1024)(128)(4,1)}), s8[1048576]{0:T(1024)(128)(4,1)S(1)}, s32[]{:S(2)}) async-start(s8[9437184]{0:T(1024)(128)(4,1)} %bitcast.266), calls=%async_computation.3 | async-start | bytes 2097152
  261.5 13.9 %copy-start.9 = (f32[1,6,256,256]{3,2,1,0:T(8,128)S(1)}, f32[1,6,256,256]{3,2,1,0:T(8,128)}, u32[]{:S(2)}) copy-start(f32[1,6,256,256]{3,2,1,0:T(8,128)} %copy.145) | copy-start | bytes 4718596
  277.9 4.3 %collective-permute-start.7 = (bf16[4,1,2,128,256]{4,3,2,1,0:T(8,128)(2,1)S(1)}, bf16[4,1,2,128,256]{4,3,2,1,0:T(8,128)(2,1)S(1)}, u32[]{:S(2)}, u32[]{:S(2)}) collective-permute-start(bf16[4,1,2,128,256]{4,3,2,1,0:T(8,128)(2,1)S(1)} %get-tuple-element.78), channel_id=1, source_target_pairs={{1,0},{0,1},{3,2},{2,3},{5,4},{4,5},{7,6},{6,7},{9,8},{8,9},{11,10... | collective-permute-start | bytes 1572872 | tf_op jit(solution)/shard_map/ppermute | solution.py:18
  278.0 4.3 %collective-permute-start.6 = (bf16[4,1,2,128,256]{4,3,2,1,0:T(8,128)(2,1)S(1)}, bf16[4,1,2,128,256]{4,3,2,1,0:T(8,128)(2,1)S(1)}, u32[]{:S(2)}, u32[]{:S(2)}) collective-permute-start(bf16[4,1,2,128,256]{4,3,2,1,0:T(8,128)(2,1)S(1)} %get-tuple-element.77), channel_id=1, source_target_pairs={{0,1},{1,0},{2,3},{3,2},{4,5},{5,4},{6,7},{7,6},{8,9},{9,8},{10,11... | collective-permute-start | bytes 1572872 | tf_op jit(solution)/shard_map/ppermute | solution.py:16
  282.3 2.2 copy-start.3
Sparse Core Ops, SparseCore 0:
  24.4 36.9 all-gather.1
where the time goes:
time: 301 us; the launch traced here: 296 us
  other arithmetic  91.3 us (30%)
  local copies, waits for them, and re-layouts  86.9 us (29%)
  matrix products  77.8 us (26%)
  between operations  14.9 us (5%)
  waiting for transfers between devices  13.1 us (4%)
  starting transfers between devices  11.7 us (4%)
    unnamed x58, local copies, waits for them, and re-layouts  55.7 us
    concatenate x3, other arithmetic, combine_planes(): return jnp.concatenate([real, imag], axis=1)  23.1 us
    sub x3, other arithmetic, combine_planes(): real = raw[:, 0, :half] - raw[:, 1, half:]  16.4 us
    add x3, other arithmetic, combine_planes(): imag = raw[:, 0, half:] + raw[:, 1, :half]  16.3 us
    dot_general x1, matrix products, per_device(): jnp.dot(col_hot.T, transposed.reshape(width, -1), precision=HIGH)  14.9 us
    dot_general x1, matrix products, per_device(): jnp.einsum('scpq,sjp->scjq', near_mats, row_source, preferred_element_typ...  14.7 us
    dot_general x1, matrix products, per_device(): jnp.einsum('scpq,sjq->scjp', near_mats, column_source, preferred_element_...  12.8 us
    ppermute x4, waiting for transfers between devices, extended_2(): lax.ppermute(head, axis, [((i + 1) % count, i) for i in range(count)])  12.8 us
  transfers between devices with their start and end apart: 9, of which 3 were waited for; matrix products, arithmetic and copies ran while one was open for 82% of the time, Pallas kernels for 0%

commit v1 on v0

v1 whole, which is shorter than its diff:
```python
import functools

import jax
import jax.numpy as jnp
from jax import lax
from jax.experimental import pallas as pl
from jax.experimental.pallas import tpu as pltpu
from jax.sharding import PartitionSpec as P

F32 = jnp.float32
BF16 = jnp.bfloat16
RING = 6
VMEM_LIMIT = 48 * 1024 * 1024


def dot_nn(a, b):
    return lax.dot_general(a, b, (((1,), (0,)), ((), ())), preferred_element_type=F32)


def dot_nt(a, b):
    return lax.dot_general(a, b, (((1,), (1,)), ((), ())), preferred_element_type=F32)


def dot_tn(a, b):
    return lax.dot_general(a, b, (((0,), (0,)), ((), ())), preferred_element_type=F32)


def add_planes(acc, at, raw_r, raw_i, half, fresh=False):
    real = raw_r[:half] - raw_i[half:]
    imag = raw_r[half:] + raw_i[:half]
    if fresh:
        acc[at, :half, :] = real
        acc[at, half:, :] = imag
    else:
        acc[at, :half, :] += real
        acc[at, half:, :] += imag


def turned(value, cos, sin, half):
    re = value[:half].astype(F32)
    im = value[half:].astype(F32)
    return cos * re - sin * im, sin * re + cos * im


def slot_place(pairs, s, tile_y):
    r = pairs[2 * s]
    d = pairs[2 * s + 1]
    u = d + jnp.where(d >= 4, 1, 0)
    ux = jnp.where(u >= 6, 2, jnp.where(u >= 3, 1, 0))
    rx = lax.div(r, tile_y)
    ry = r - rx * tile_y
    return r, rx + ux, ry + u - 3 * ux


def pick_slots(pairs, count, chosen, tile_x, tile_y, crossing):
    def one(s, found):
        _, cx, _ = slot_place(pairs, s, tile_y)
        over = (cx == 0) | (cx == tile_x + 1)
        take = over if crossing else jnp.logical_not(over)

        @pl.when(take)
        def _():
            chosen[found] = s

        return found + jnp.where(take, 1, 0)

    return lax.fori_loop(0, count, one, 0)


def out_kernel(tile_x, tile_y, half, pairs, count, cos, sin, own, near, main, corner, chosen, acc, ring, sems):
    wide_y = tile_y + 2
    n = pick_slots(pairs, count[0], chosen, tile_x, tile_y, True)

    def copy(t):
        return pltpu.make_async_copy(near.at[chosen[t]], ring.at[lax.rem(t, RING)], sems.at[lax.rem(t, RING)])

    def start(t):
        @pl.when(t < n)
        def _():
            copy(t).start()

    for t in range(RING - 1):
        start(t)
    acc[...] = jnp.zeros_like(acc)

    def body(t, carry):
        copy(t).wait()
        start(t + RING - 1)
        mats = ring.at[lax.rem(t, RING)]
        r, cx, cy = slot_place(pairs, chosen[t], tile_y)
        x = own[r]
        at = jnp.where(cx == 0, 0, wide_y) + cy
        add_planes(acc, at, dot_nn(x, mats[0]), dot_nn(x, mats[1]), half)
        return carry

    lax.fori_loop(0, n, body, 0)
    for side in range(2):
        for cy in range(wide_y):
            w = (tile_x + 1) * side * wide_y + cy
            re, im = turned(acc.at[side * wide_y + cy], cos[w], -sin[w], half)
            if 0 < cy < wide_y - 1:
                main[side, cy - 1, :half, :] = re.astype(BF16)
                main[side, cy - 1, half:, :] = im.astype(BF16)
            else:
                corner[side, min(cy, 1), :half, :] = re.astype(BF16)
                corner[side, min(cy, 1), half:, :] = im.astype(BF16)


def fold_kernel(tile_y, main, corner, left, right):
    for side, out in ((0, left), (1, right)):
        for j in range(tile_y):
            total = main[side, j].astype(F32)
            if j == tile_y - 1:
                total = total + corner[side, 0].astype(F32)
            if j == 0:
                total = total + corner[side, 1].astype(F32)
            out[j] = total.astype(BF16)


def leaf_kernel(blocks, rank, half, parent, own, basis, moves, coeff, acc):
    acc[...] = jnp.zeros_like(acc)
    for b in range(blocks):
        raw = dot_nt(basis[b], own[b])
        real = raw[:rank, :half] - raw[rank:, half:]
        imag = raw[:rank, half:] + raw[rank:, :half]
        leaf = jnp.concatenate([real, imag], axis=0)
        high = leaf.astype(BF16)
        low = (leaf - high.astype(F32)).astype(BF16)
        acc[parent[b]] += dot_nn(moves[b], high) + dot_nn(moves[b], low)
    for q in range(acc.shape[0]):
        coeff[q * rank : (q + 1) * rank, :half] = acc[q, :rank].astype(BF16)
        coeff[q * rank : (q + 1) * rank, half:] = acc[q, rank:].astype(BF16)


def inner_kernel(
    tile_x, tile_y, half, pairs, count, cos, sin, own, beside, own_mats, near, total, back, chosen, win, acc, ring, sems, own_sem
):
    blocks = tile_x * tile_y
    wide_y = tile_y + 2
    fetch = pltpu.make_async_copy(own, win.at[pl.ds(0, blocks)], own_sem)
    fetch.start()
    n = pick_slots(pairs, count[0], chosen, tile_x, tile_y, False)

    def wait(t):
        pltpu.make_async_copy(near.at[0], ring.at[lax.rem(t, RING)], sems.at[lax.rem(t, RING)]).wait()

    def start(t):
        to, sem = ring.at[lax.rem(t, RING)], sems.at[lax.rem(t, RING)]

        @pl.when(t < blocks)
        def _():
            pltpu.make_async_copy(own_mats.at[t], to, sem).start()

        @pl.when((t >= blocks) & (t < blocks + n))
        def _():
            pltpu.make_async_copy(near.at[chosen[jnp.maximum(t - blocks, 0)]], to, sem).start()

    for t in range(RING - 1):
        start(t)
    acc[blocks:] = jnp.zeros((2 * tile_x,) + acc.shape[1:], F32)
    for side in range(2):
        for i in range(tile_x):
            w = (i + 1) * wide_y + side * (wide_y - 1)
            re, im = turned(beside.at[1 - side, i], cos[w], sin[w], half)
            win[blocks + side * tile_x + i, :half, :] = re.astype(BF16)
            win[blocks + side * tile_x + i, half:, :] = im.astype(BF16)
    fetch.wait()

    def own_body(t, carry):
        wait(t)
        start(t + RING - 1)
        mats = ring.at[lax.rem(t, RING)]
        x = win[t]
        add_planes(acc, t, dot_nt(x, mats[0]), dot_nt(x, mats[1]), half, True)
        return carry

    lax.fori_loop(0, blocks, own_body, 0)

    def near_body(t, carry):
        wait(t)
        start(t + RING - 1)
        mats = ring.at[lax.rem(t, RING)]
        r, cx, cy = slot_place(pairs, chosen[t - blocks], tile_y)
        inside = (cx - 1) * tile_y + cy - 1
        c = jnp.where(cy == 0, blocks + cx - 1, jnp.where(cy == wide_y - 1, blocks + tile_x + cx - 1, inside))
        x = win[c]
        add_planes(acc, r, dot_nt(x, mats[0]), dot_nt(x, mats[1]), half)
        x = win[r]
        add_planes(acc, c, dot_nn(x, mats[0]), dot_nn(x, mats[1]), half)
        return carry

    lax.fori_loop(blocks, blocks + n, near_body, 0)
    for side in range(2):
        for i in range(tile_x):
            w = (i + 1) * wide_y + side * (wide_y - 1)
            re, im = turned(acc.at[blocks + side * tile_x + i], cos[w], -sin[w], half)
            back[side, i, :half, :] = re.astype(BF16)
            back[side, i, half:, :] = im.astype(BF16)
    total[...] = acc[:blocks]


def far_kernel(
    tile_x, tile_y, half, rank, pieces, pairs, count, cos, sin, parent, place, near_total, back, coeff, other, coupling, moves,
    basis, from_left, from_right, corner, near, out, edge, chosen, win, acc, far, stage, ring, sems, out_sem
):
    blocks = tile_x * tile_y
    wide_y = tile_y + 2
    n = pick_slots(pairs, count[0], chosen, tile_x, tile_y, True)

    def copy(t):
        return pltpu.make_async_copy(near.at[chosen[t]], ring.at[lax.rem(t, RING)], sems.at[lax.rem(t, RING)])

    def start(t):
        @pl.when(t < n)
        def _():
            copy(t).start()

    for t in range(RING - 1):
        start(t)

    for side in range(2):
        for cy in range(wide_y):
            w = (tile_x + 1) * side * wide_y + cy
            if cy == 0:
                cell = corner.at[side, 1]
            elif cy == wide_y - 1:
                cell = corner.at[side, 0]
            else:
                cell = (from_left, from_right)[side].at[cy - 1]
            re, im = turned(cell, cos[w], sin[w], half)
            win[side * wide_y + cy, :half, :] = re.astype(BF16)
            win[side * wide_y + cy, half:, :] = im.astype(BF16)

    raw = jnp.zeros((acc.shape[1], 2 * half), F32)
    rows = coeff.shape[0] // pieces
    for source, mine in ((coeff, True), (other, False)):
        for k in range(pieces):
            tile = jnp.bitwise_xor(place[0], k) * 2 + (place[1] if mine else 1 - place[1])
            raw = raw + dot_nn(coupling[tile], source[k * rows : (k + 1) * rows, :])
    for p in range(far.shape[0]):
        top = raw[2 * rank * p : 2 * rank * p + rank]
        low = raw[2 * rank * p + rank : 2 * rank * (p + 1)]
        far[p, :rank, :] = top[:, :half] - low[:, half:]
        far[p, rank:, :] = -(top[:, half:] + low[:, :half])

    def block(b):
        chosen_far = far[parent[b]].astype(BF16)
        down = dot_tn(moves[b], chosen_far).astype(BF16)
        both = jnp.concatenate([down, jnp.concatenate([-down[rank:], down[:rank]], axis=0)], axis=1)
        value = dot_tn(both, basis[b]) + near_total[b]
        j = b % tile_y
        if j == tile_y - 1:
            value = value + back[0, b // tile_y].astype(F32)
        if j == 0:
            value = value + back[1, b // tile_y].astype(F32)
        return value

    inner = (tile_x - 2) * tile_y
    for b in range(tile_y, blocks - tile_y):
        stage[b - tile_y] = block(b).astype(BF16)
    put = pltpu.make_async_copy(stage, out.at[pl.ds(tile_y, inner)], out_sem)
    put.start()
    for j in range(tile_y):
        acc[j] = block(j)
        acc[tile_y + j] = block(blocks - tile_y + j)

    def body(t, carry):
        copy(t).wait()
        start(t + RING - 1)
        mats = ring.at[lax.rem(t, RING)]
        r, cx, cy = slot_place(pairs, chosen[t], tile_y)
        x = win[jnp.where(cx == 0, 0, wide_y) + cy]
        at = jnp.where(cx == 0, r, r - (tile_x - 2) * tile_y)
        add_planes(acc, at, dot_nt(x, mats[0]), dot_nt(x, mats[1]), half)
        return carry

    lax.fori_loop(0, n, body, 0)
    edge[...] = acc[...]
    put.wait()


def last_kernel(tile_x, tile_y, edge, to_first, to_last, unused, out, stage, sems):
    blocks = tile_x * tile_y
    del unused
    puts = []
    for side, came in ((0, to_first), (1, to_last)):
        for j in range(tile_y):
            stage[side, j] = (edge[side * tile_y + j] + came[j].astype(F32)).astype(BF16)
        put = pltpu.make_async_copy(stage.at[side], out.at[pl.ds(side * (blocks - tile_y), tile_y)], sems.at[side])
        put.start()
        puts.append(put)
    for put in puts:
        put.wait()


SMEM = pl.BlockSpec(memory_space=pltpu.SMEM)
VMEM = pl.BlockSpec(memory_space=pltpu.VMEM)
ANY = pl.BlockSpec(memory_space=pl.ANY)


def call(kernel, ins, in_specs, outs, out_specs, scratch, flops, moved, name, aliases=None):
    return pl.pallas_call(
        kernel,
        out_shape=outs,
        in_specs=in_specs,
        out_specs=out_specs,
        scratch_shapes=scratch,
        input_output_aliases=aliases or {},
        compiler_params=pltpu.CompilerParams(vmem_limit_bytes=VMEM_LIMIT),
        cost_estimate=pl.CostEstimate(flops=flops, bytes_accessed=moved, transcendentals=0),
        name=name,
    )(*ins)


def per_device(
    currents, self_blocks, near_blocks, near_pairs, near_count, basis, transfer, coupling, far_shift, far_mask, parent, bloch
):
    tile_x, tile_y, _, half, panels = currents.shape
    rank = basis.shape[3]
    blocks = tile_x * tile_y
    wide_x, wide_y = tile_x + 2, tile_y + 2
    gx_count, gy_count = lax.axis_size("gx"), lax.axis_size("gy")
    gx_index, gy_index = lax.axis_index("gx"), lax.axis_index("gy")
    clusters = far_mask.shape[0]
    tiles = gx_count * gy_count
    width = 2 * half
    slots = near_pairs.shape[2]

    def shape(*dims, dtype=BF16):
        return jax.ShapeDtypeStruct(dims, dtype)

    right = [(i, (i + 1) % gx_count) for i in range(gx_count)]
    left = [((i + 1) % gx_count, i) for i in range(gx_count)]
    swap = [(i, (i + 1) % gy_count) for i in range(gy_count)]

    own = currents.reshape(blocks, width, panels)
    from_left = lax.ppermute(own[blocks - tile_y :], "gx", right)
    from_right = lax.ppermute(own[:tile_y], "gx", left)
    columns = jnp.stack([currents[:, 0], currents[:, tile_y - 1]]).reshape(2, tile_x, width, panels)
    beside = lax.ppermute(columns, "gy", swap)

    pairs = near_pairs.reshape(2 * slots)
    count = near_count.reshape(1)
    near = near_blocks.reshape(slots, 2, panels, panels)
    own_mats = self_blocks.reshape(blocks, 2, panels, panels)
    steps_x = jnp.zeros((wide_x,), F32).at[0].set(jnp.where(gx_index == 0, -1.0, 0.0))
    steps_x = steps_x.at[wide_x - 1].set(jnp.where(gx_index == gx_count - 1, 1.0, 0.0))
    steps_y = jnp.zeros((wide_y,), F32).at[0].set(jnp.where(gy_index == 0, -1.0, 0.0))
    steps_y = steps_y.at[wide_y - 1].set(jnp.where(gy_index == gy_count - 1, 1.0, 0.0))
    phases = (bloch[0] * steps_x[:, None] + bloch[1] * steps_y[None, :]).reshape(-1)
    cos, sin = jnp.cos(phases), jnp.sin(phases)
    cluster_base = (gx_index * gy_count + gy_index) * clusters
    local_parent = parent.reshape(blocks) - cluster_base
    basis_b = basis.reshape(blocks, 2 * rank, panels)
    tr = transfer.reshape(blocks, 2, rank, rank)
    moves = jnp.concatenate(
        [jnp.concatenate([tr[:, 0], -tr[:, 1]], axis=2), jnp.concatenate([tr[:, 1], tr[:, 0]], axis=2)], axis=1
    )

    coeff = call(
        functools.partial(leaf_kernel, blocks, rank, half),
        (local_parent, own, basis_b, moves),
        [SMEM, VMEM, VMEM, VMEM],
        shape(clusters * rank, width),
        VMEM,
        [pltpu.VMEM((clusters, 2 * rank, half), F32)],
        2 * blocks * 2 * rank * panels * width,
        own.size * 2 + basis_b.size * 2,
        "leaf",
    )
    main, corner = call(
        functools.partial(out_kernel, tile_x, tile_y, half),
        (pairs, count, cos, sin, own, near),
        [SMEM, SMEM, SMEM, SMEM, VMEM, ANY],
        [shape(2, tile_y, width, panels), shape(2, 2, width, panels)],
        [VMEM, VMEM],
        [
            pltpu.SMEM((slots,), jnp.int32),
            pltpu.VMEM((2 * wide_y, width, panels), F32),
            pltpu.VMEM((RING, 2, panels, panels), BF16),
            pltpu.SemaphoreType.DMA((RING,)),
        ],
        2 * 10 * 2 * width * panels * panels,
        own.size * 2 + 10 * 2 * 2 * panels * panels,
        "outward",
    )
    corner_in = lax.ppermute(corner, "gy", swap)
    back_left, back_right = call(
        functools.partial(fold_kernel, tile_y),
        (main, corner_in),
        [VMEM, VMEM],
        [shape(tile_y, width, panels), shape(tile_y, width, panels)],
        [VMEM, VMEM],
        [],
        main.size,
        main.size * 6,
        "fold",
    )
    to_last = lax.ppermute(back_left, "gx", left)
    to_first = lax.ppermute(back_right, "gx", right)

    bit = 1
    while bit < gx_count:
        other = lax.ppermute(coeff, "gx", [(i, i ^ bit) for i in range(gx_count)])
        coeff = jnp.concatenate([coeff, other], axis=0)
        bit *= 2
    other = lax.ppermute(coeff, "gy", swap)

    near_total, y_back = call(
        functools.partial(inner_kernel, tile_x, tile_y, half),
        (pairs, count, cos, sin, own, beside, own_mats, near),
        [SMEM, SMEM, SMEM, SMEM, ANY, VMEM, ANY, ANY],
        [shape(blocks, width, panels, dtype=F32), shape(2, tile_x, width, panels)],
        [VMEM, VMEM],
        [
            pltpu.SMEM((slots,), jnp.int32),
            pltpu.VMEM((blocks + 2 * tile_x, width, panels), BF16),
            pltpu.VMEM((blocks + 2 * tile_x, width, panels), F32),
            pltpu.VMEM((RING, 2, panels, panels), BF16),
            pltpu.SemaphoreType.DMA((RING,)),
            pltpu.SemaphoreType.DMA,
        ],
        2 * (2 * slots * 3 // 4 + blocks) * 2 * width * panels * panels,
        near.size * 2 + own_mats.size * 2 + own.size * 8,
        "inner",
    )
    back = lax.ppermute(y_back, "gy", swap)

    pair_phase = bloch[0] * far_shift[..., 0].astype(F32) + bloch[1] * far_shift[..., 1].astype(F32)
    keep = far_mask.astype(F32)
    weight_cos = (keep * jnp.cos(pair_phase)).reshape(clusters, tiles, clusters, 1, 1)
    weight_sin = (keep * jnp.sin(pair_phase)).reshape(clusters, tiles, clusters, 1, 1)
    mats = coupling.reshape(clusters, tiles, clusters, 2, rank, rank).astype(F32)
    mats = jnp.stack(
        [
            weight_cos * mats[:, :, :, 0] - weight_sin * mats[:, :, :, 1],
            weight_sin * mats[:, :, :, 0] + weight_cos * mats[:, :, :, 1],
        ],
        axis=3,
    ).astype(BF16)
    mats = mats.transpose(1, 0, 3, 4, 2, 5).reshape(tiles, clusters * 2 * rank, clusters * rank)

    halo_corner = jnp.stack(
        [from_left[0], from_left[tile_y - 1], from_right[0], from_right[tile_y - 1]]
    ).reshape(2, 2, width, panels)
    halo_corner = lax.ppermute(halo_corner, "gy", swap)
    place = jnp.stack([gx_index, gy_index]).astype(jnp.int32)
    out, edge = call(
        functools.partial(far_kernel, tile_x, tile_y, half, rank, gx_count),
        (
            pairs, count, cos, sin, local_parent, place, near_total, back, coeff, other, mats, moves, basis_b, from_left,
            from_right, halo_corner, near,
        ),
        [SMEM] * 6 + [VMEM] * 10 + [ANY],
        [shape(blocks, width, panels), shape(2 * tile_y, width, panels, dtype=F32)],
        [ANY, VMEM],
        [
            pltpu.SMEM((slots,), jnp.int32),
            pltpu.VMEM((2 * wide_y, width, panels), BF16),
            pltpu.VMEM((2 * tile_y, width, panels), F32),
            pltpu.VMEM((clusters, 2 * rank, half), F32),
            pltpu.VMEM(((tile_x - 2) * tile_y, width, panels), BF16),
            pltpu.VMEM((RING, 2, panels, panels), BF16),
            pltpu.SemaphoreType.DMA((RING,)),
            pltpu.SemaphoreType.DMA,
        ],
        2 * 20 * 2 * width * panels * panels,
        near_total.size * 4 + coupling.size * 2 + own.size * 4 + 10 * 2 * 2 * panels * panels,
        "far",
    )
    out = call(
        functools.partial(last_kernel, tile_x, tile_y),
        (edge, to_first, to_last, out),
        [VMEM, VMEM, VMEM, ANY],
        shape(blocks, width, panels),
        ANY,
        [pltpu.VMEM((2, tile_y, width, panels), BF16), pltpu.SemaphoreType.DMA((2,))],
        edge.size,
        edge.size * 8,
        "last",
        aliases={3: 0},
    )
    return out.reshape(currents.shape)


def solution(mesh):
    placed = (
        P(("groups", "gx"), "gy", None, None, None),
        P(("groups", "gx"), "gy", None, None, None),
        P(("groups", "gx"), "gy", None, None, None, None),
        P(("groups", "gx"), "gy", None, None),
        P(("groups", "gx"), "gy"),
        P(("groups", "gx"), "gy", None, None, None),
        P(("groups", "gx"), "gy", None, None),
        P(("groups", "gx", "gy"), None, None, None),
        P(("groups", "gx", "gy"), None, None),
        P(("groups", "gx", "gy"), None),
        P(("groups", "gx"), "gy"),
        P("groups"),
    )
    return jax.shard_map(
        per_device,
        mesh=mesh,
        in_specs=placed,
        out_specs=P(("groups", "gx"), "gy", None, None, None),
        check_vma=False,
    )
```

time: 301 us -> 118 us (0.39)
  the two profiles are of different devices: /device:TPU:0 before, /device:TPU:26 now
where the time goes in v1:
time: 118 us
  Pallas kernels  48.6 us (41%)
  local copies, waits for them, and re-layouts  29.3 us (25%)
  other arithmetic  22.6 us (19%)
  starting transfers between devices  9.3 us (8%)
  waiting for transfers between devices  7.23 us (6%)
  between operations  1.18 us (1%)
    pallas_call x6, Pallas kernels, call(): pl.pallas_call(kernel, out_shape=outs, in_specs=in_specs, out_specs=out_s...  48.6 us
    another operation x1, other arithmetic  11.5 us
    slice x1, local copies, waits for them, and re-layouts, per_device(): mats[:, :, :, 0]  8.65 us
    ppermute x3, waiting for transfers between devices, per_device(): other = lax.ppermute(coeff, 'gx', [(i, i ^ bit) for i in range(gx_count)])  7.21 us
    convert_element_type x1, local copies, waits for them, and re-layouts, per_device(): coupling.reshape(clusters, tiles, clusters, 2, rank, rank).astype(F32)  6.72 us
    transpose x1, other arithmetic, per_device(): mats.transpose(1, 0, 3, 4, 2, 5)  5.32 us
    reshape x1, local copies, waits for them, and re-layouts, per_device(): mats.transpose(1, 0, 3, 4, 2, 5)  5.21 us
    ppermute x1, starting transfers between devices, per_device(): to_last = lax.ppermute(back_left, 'gx', left)  2.92 us
  transfers between devices with their start and end apart: 12, of which 2 were waited for; matrix products, arithmetic and copies ran while one was open for 40% of the time, Pallas kernels for 39%

profile of v1, /device:TPU:26, one launch (start us, length us, event | category | flops | bytes accessed | tf_op | source)
XLA Modules:
  0.0 118.2 jit_solution(892414202790662920)
XLA Ops:
  0.0 1.4 %fusion.3 = (bf16[4,1,2,128,256]{4,3,2,1,0:T(8,128)(2,1)S(1)}, bf16[4,1,2,128,256]{4,3,2,1,0:T(8,128)(2,1)S(1)}) fusion(bf16[4,4,2,128,256]{4,3,2,1,0:T(8,128)(2,1)} %param.20), kind=kLoop, calls=%fused_computation.25 | loop fusion | bytes 2097152 | tf_op jit(solution)/shard_map/slice | solution.py:339
  1.5 1.1 pad_maximum_fusion
  2.6 0.2 reshape.158
  3.1 3.1 %leaf.1 = bf16[128,256]{1,0:T(8,128)(2,1)S(1)} custom-call(s32[16]{0:T(128)S(1)} %sub.14.parent, bf16[16,256,256]{2,1,0:T(8,128)(2,1)S(1)} %bitcast.48, bf16[16,64,256]{2,1,0:T(8,128)(2,1)S(1)} %bitcast.51, bf16[16,64,64]{2,1,0:T(8,128)(2,1)S(1)} %maximum_maximum_fusion.moves), custom_call_target="tpu_custom_call" | custom-call | flops 134217728 | bytes 2621440 | tf_op jit(solution)/shard_map/leaf/pallas_call | solution.py:302
  6.3 1.6 %collective-permute-start.2 = (bf16[128,256]{1,0:T(8,128)(2,1)S(1)}, bf16[128,256]{1,0:T(8,128)(2,1)S(1)}, u32[]{:S(2)}, u32[]{:S(2)}) collective-permute-start(bf16[128,256]{1,0:T(8,128)(2,1)S(1)} %leaf.1), channel_id=1, source_target_pairs={{0,2},{2,0},{4,6},{6,4},{8,10},{10,8},{12,14},{14,12},{1,3},{3,1},... | collective-permute-start | bytes 196616 | tf_op jit(solution)/shard_map/ppermute | solution.py:404
  7.9 1.0 fusion.2
  8.9 0.5 collective-permute-start.6
  9.4 2.4 %collective-permute-start.7 = (bf16[4,256,256]{2,1,0:T(8,128)(2,1)}, bf16[4,256,256]{2,1,0:T(8,128)(2,1)}, u32[]{:S(2)}, u32[]{:S(2)}) collective-permute-start(bf16[4,256,256]{2,1,0:T(8,128)(2,1)} %bitcast.25), channel_id=1, source_target_pairs={{2,0},{4,2},{6,4},{8,6},{10,8},{12,10},{14,12},{0,14},{3,1},{5,3},... | collective-permute-start | bytes 1572872 | tf_op jit(solution)/shard_map/ppermute | solution.py:338
  12.7 0.6 fusion.7
  13.4 0.6 multiply_bitcast_fusion
  14.1 0.6 multiply_bitcast_fusion.1
  15.0 6.2 %outward.1 = (bf16[2,4,256,256]{3,2,1,0:T(8,128)(2,1)S(1)}, bf16[2,2,256,256]{3,2,1,0:T(8,128)(2,1)}) custom-call(s32[80]{0:T(128)S(1)} %reshape.150.pairs, s32[1]{0:T(128)} %bitcast.47.count, f32[36]{0:T(128)S(1)} %cos.13, f32[36]{0:T(128)S(1)} %sin.13, bf16[16,256,256]{2,1,0:T(8,128)(2,1)S(1)} %bitcast.49, bf16[40,2,256,256]{3,2,1,0:T(8,128)(2,1)} %bitcast.53), custom_call_target="tpu_custom_call" | custom-call | flops 671088640 | bytes 4718592 | tf_op jit(solution)/shard_map/outward/pallas_call | solution.py:302
  21.2 1.0 copy-done.3
  22.2 6.7 %reshape.162 = f32[4,16,4,2,32,32]{5,4,3,2,1,0:T(8,128)} reshape(bf16[4,64,2,1024]{3,2,1,0:T(2,128)(2,1)} %param.27) | data formatting | bytes 3145728 | tf_op jit(solution)/shard_map/convert_element_type | solution.py:433
  28.9 8.7 %fusion.1 = (f32[4,16,4,1,32,32]{5,4,3,2,1,0:T(8,128)}, f32[4,16,4,1,32,32]{5,4,3,2,1,0:T(8,128)}) fusion(f32[4,16,4,2,32,32]{5,4,3,2,1,0:T(8,128)} %reshape.162), kind=kLoop, calls=%fused_computation.23 | loop fusion | bytes 4194304 | tf_op jit(solution)/shard_map/slice | solution.py:436
  37.7 1.2 %bitcast_multiply_fusion.1 = (f32[4,64]{1,0:T(4,128)S(1)}, f32[4,64]{1,0:T(4,128)S(1)}) fusion(s32[4,64]{1,0:T(4,128)S(1)} %copy-done.10, s32[4,64,1]{1,0,2:T(4,128)S(1)} %bitcast.59, f32[]{:T(128)} %bitcast.6, s32[4,64,1]{1,0,2:T(4,128)S(1)} %bitcast.58, f32[]{:T(128)} %bitcast.1), kind=kLoop, calls=%fused_computation.14 | loop fusion | flops 2048 | bytes 5128 | tf_op jit(solution)/shard_map/mul | solution.py:431
  39.2 4.4 %collective-permute-done.3 = bf16[256,256]{1,0:T(8,128)(2,1)S(1)} collective-permute-done((bf16[256,256]{1,0:T(8,128)(2,1)S(1)}, bf16[256,256]{1,0:T(8,128)(2,1)S(1)}, u32[]{:S(2)}, u32[]{:S(2)}) %collective-permute-start.3) | collective-permute-done | bytes 131104 | tf_op jit(solution)/shard_map/ppermute | solution.py:404
  43.7 11.5 %subtract_convert_fusion = (bf16[4,16,4,1,32,32]{5,2,4,3,0,1:T(4,128)(2,1)S(1)}, bf16[4,16,4,1,32,32]{5,2,4,3,0,1:T(4,128)(2,1)S(1)}) fusion(f32[4,16,4,1,32,32]{5,4,3,2,1,0:T(8,128)} %get-tuple-element.72, f32[4,16,4,1,32,32]{5,4,3,2,1,0:T(8,128)} %get-tuple-element.71, f32[4,16,4]{2,0,1:T(4,128)S(1)} %copy.28, f32[4,16,4]{2,0,1:T(4,128)S(1)} %copy.26), kind=kLoop, calls=%fused_computation.2 | loop fusion | flops 2097152 | bytes 3147776 | tf_op jit(solution)/shard_map/convert.1
  55.3 2.8 %collective-permute-done.4 = bf16[512,256]{1,0:T(8,128)(2,1)S(1)} collective-permute-done((bf16[512,256]{1,0:T(8,128)(2,1)S(1)}, bf16[512,256]{1,0:T(8,128)(2,1)S(1)}, u32[]{:S(2)}, u32[]{:S(2)}) %collective-permute-start.4) | collective-permute-done | bytes 262176 | tf_op jit(solution)/shard_map/ppermute | solution.py:404
  58.1 0.9 pad_maximum_fusion.1.coeff
  59.1 20.7 %inner.1 = (f32[16,256,256]{2,1,0:T(8,128)}, bf16[2,4,256,256]{3,2,1,0:T(8,128)(2,1)}) custom-call(s32[80]{0:T(128)S(1)} %reshape.150.pairs, s32[1]{0:T(128)} %bitcast.45.count, f32[36]{0:T(128)S(1)} %cos.13, f32[36]{0:T(128)S(1)} %sin.13, bf16[16,256,256]{2,1,0:T(8,128)(2,1)S(1)} %bitcast.50, bf16[2,4,256,256]{3,2,1,0:T(8,128)(2,1)} %collective-permute-done.beside, ...), custom_call_target="tpu_custom_call" | custom-call | flops 5100273664 | bytes 23068672 | tf_op jit(solution)/shard_map/inner/pallas_call | solution.py:302
  79.8 1.6 %collective-permute-start.1 = (bf16[2,4,256,256]{3,2,1,0:T(8,128)(2,1)}, bf16[2,4,256,256]{3,2,1,0:T(8,128)(2,1)S(1)}, u32[]{:S(2)}, u32[]{:S(2)}) collective-permute-start(bf16[2,4,256,256]{3,2,1,0:T(8,128)(2,1)} %get-tuple-element.62), channel_id=1, source_target_pairs={{0,1},{1,0},{2,3},{3,2},{4,5},{5,4},{6,7},{7,6},{8,9},{9,8},{10,11... | collective-permute-start | bytes 3145736 | tf_op jit(solution)/shard_map/ppermute | solution.py:427
  81.4 1.0 fusion.5
  82.4 1.0 fusion.4
  83.4 0.9 pad_maximum_fusion.2
  84.3 2.1 %fold.1 = (bf16[4,256,256]{2,1,0:T(8,128)(2,1)}, bf16[4,256,256]{2,1,0:T(8,128)(2,1)}) custom-call(bf16[2,4,256,256]{3,2,1,0:T(8,128)(2,1)S(1)} %copy-done.4, bf16[2,2,256,256]{3,2,1,0:T(8,128)(2,1)} %collective-permute-done.9.corner), custom_call_target="tpu_custom_call" | custom-call | flops 524288 | bytes 3145728 | tf_op jit(solution)/shard_map/fold/pallas_call | solution.py:302
  86.4 2.9 %collective-permute-start.11 = (bf16[4,256,256]{2,1,0:T(8,128)(2,1)}, bf16[4,256,256]{2,1,0:T(8,128)(2,1)}, u32[]{:S(2)}, u32[]{:S(2)}) collective-permute-start(bf16[4,256,256]{2,1,0:T(8,128)(2,1)} %get-tuple-element.67), channel_id=1, source_target_pairs={{2,0},{4,2},{6,4},{8,6},{10,8},{12,10},{14,12},{0,14},{3,1},{5,3},... | collective-permute-start | bytes 1572872 | tf_op jit(solution)/shard_map/ppermute | solution.py:399
  89.3 5.3 %maximum_bitcast_fusion = bf16[16,4,2,32,4,32]{5,4,3,2,1,0:T(4,128)(2,1)} fusion(bf16[4,16,4,1,32,32]{5,2,4,3,0,1:T(4,128)(2,1)S(1)} %get-tuple-element.70, bf16[4,16,4,1,32,32]{5,2,4,3,0,1:T(4,128)(2,1)S(1)} %get-tuple-element.69), kind=kLoop, calls=%fused_computation | loop fusion | flops 524288 | bytes 2097152 | tf_op jit(solution)/shard_map/transpose | solution.py:441
  94.6 5.2 %reshape.159.coupling = bf16[16,256,128]{2,1,0:T(8,128)(2,1)S(1)} reshape(bf16[16,4,2,32,4,32]{5,4,3,2,1,0:T(4,128)(2,1)} %maximum_bitcast_fusion) | data formatting | bytes 2097152 | tf_op jit(solution)/shard_map/reshape | solution.py:441
  100.0 14.2 %far.1 = (bf16[16,256,256]{2,1,0:T(8,128)(2,1)}, f32[8,256,256]{2,1,0:T(8,128)}) custom-call(s32[80]{0:T(128)S(1)} %reshape.150.pairs, s32[1]{0:T(128)} %bitcast.46.count, f32[36]{0:T(128)S(1)} %cos.13, f32[36]{0:T(128)S(1)} %sin.13, s32[16]{0:T(128)S(1)} %sub.14.parent, s32[2]{0:T(128)S(1)} %pad_add_fusion.place, ...), custom_call_target="tpu_custom_call" | custom-call | flops 1342177280 | bytes 12058624 | tf_op jit(solution)/shard_map/far/pallas_call | solution.py:302
  114.2 1.6 %copy-done.1 = f32[8,256,256]{2,1,0:T(8,128)S(1)} copy-done((f32[8,256,256]{2,1,0:T(8,128)S(1)}, f32[8,256,256]{2,1,0:T(8,128)}, u32[]{:S(2)}) %copy-start.1) | copy-done | bytes 2097176
  115.8 2.3 %last.1 = bf16[16,256,256]{2,1,0:T(8,128)(2,1)} custom-call(f32[8,256,256]{2,1,0:T(8,128)S(1)} %copy-done.1, bf16[4,256,256]{2,1,0:T(8,128)(2,1)} %collective-permute-done.10.to_first, bf16[4,256,256]{2,1,0:T(8,128)(2,1)} %collective-permute-done.11.to_last, bf16[16,256,256]{2,1,0:T(8,128)(2,1)} %get-tuple-element.68.unused), custom_call_target="tpu_custom_call", output_to_operand_aliasing={{}: (3, {})} | custom-call | flops 524288 | bytes 4194304 | tf_op jit(solution)/shard_map/last/pallas_call | solution.py:302
  (62 shorter events, 1.6 us)
Async XLA Ops:
  0.0 3.1 %copy-start = (bf16[4,4,2,128,256]{4,3,2,1,0:T(8,128)(2,1)S(1)}, bf16[4,4,2,128,256]{4,3,2,1,0:T(8,128)(2,1)}, u32[]{:S(2)}) copy-start(bf16[4,4,2,128,256]{4,3,2,1,0:T(8,128)(2,1)} %param.20) | copy-start | bytes 6291460
  0.0 2.5 %copy-start.6 = (bf16[4,4,2,1024]{3,2,1,0:T(2,128)(2,1)S(1)}, bf16[4,4,2,1024]{3,2,1,0:T(2,128)(2,1)}, u32[]{:S(2)}) copy-start(bf16[4,4,2,1024]{3,2,1,0:T(2,128)(2,1)} %param.26) | copy-start | bytes 196612
  0.0 2.8 %copy-start.8 = (s32[4,4]{1,0:T(4,128)S(1)}, s32[4,4]{1,0:T(4,128)}, u32[]{:S(2)}) copy-start(s32[4,4]{1,0:T(4,128)} %param.30) | copy-start | bytes 196
  0.0 3.1 %copy-start.2 = (bf16[4,4,2,32,256]{4,3,2,1,0:T(8,128)(2,1)S(1)}, bf16[4,4,2,32,256]{4,3,2,1,0:T(8,128)(2,1)}, u32[]{:S(2)}) copy-start(bf16[4,4,2,32,256]{4,3,2,1,0:T(8,128)(2,1)} %param.25) | copy-start | bytes 1572868
  1.4 10.4 %copy-start.11 = (s32[1,1,40,2]{2,3,1,0:T(2,128)S(1)}, s32[1,1,40,2]{2,3,1,0:T(2,128)}, u32[]{:S(2)}) copy-start(s32[1,1,40,2]{2,3,1,0:T(2,128)} %param.23) | copy-start | bytes 964
  1.5 11.3 %copy-start.9 = (f32[2]{0:T(128)S(1)}, f32[2]{0:T(128)}, u32[]{:S(2)}) copy-start(f32[2]{0:T(128)} %param.31) | copy-start | bytes 28
  2.5 56.6 %collective-permute-start = (bf16[2,4,256,256]{3,2,1,0:T(8,128)(2,1)}, bf16[2,4,256,256]{3,2,1,0:T(8,128)(2,1)}, u32[]{:S(2)}, u32[]{:S(2)}) collective-permute-start(bf16[2,4,256,256]{3,2,1,0:T(8,128)(2,1)} %pad_maximum_fusion), channel_id=1, source_target_pairs={{0,1},{1,0},{2,3},{3,2},{4,5},{5,4},{6,7},{7,6},{8,9},{9,8},{10,11... | collective-permute-start | bytes 3145736 | tf_op jit(solution)/shard_map/ppermute | solution.py:340
  6.3 31.3 %collective-permute-start.2 = (bf16[128,256]{1,0:T(8,128)(2,1)S(1)}, bf16[128,256]{1,0:T(8,128)(2,1)S(1)}, u32[]{:S(2)}, u32[]{:S(2)}) collective-permute-start(bf16[128,256]{1,0:T(8,128)(2,1)S(1)} %leaf.1), channel_id=1, source_target_pairs={{0,2},{2,0},{4,6},{6,4},{8,10},{10,8},{12,14},{14,12},{1,3},{3,1},... | collective-permute-start | bytes 196616 | tf_op jit(solution)/shard_map/ppermute | solution.py:404
  8.9 73.5 %collective-permute-start.6 = (bf16[4,256,256]{2,1,0:T(8,128)(2,1)}, bf16[4,256,256]{2,1,0:T(8,128)(2,1)}, u32[]{:S(2)}, u32[]{:S(2)}) collective-permute-start(bf16[4,256,256]{2,1,0:T(8,128)(2,1)} %bitcast.24), channel_id=1, source_target_pairs={{0,2},{2,4},{4,6},{6,8},{8,10},{10,12},{12,14},{14,0},{1,3},{3,5},... | collective-permute-start | bytes 1572872 | tf_op jit(solution)/shard_map/ppermute | solution.py:337
  9.4 72.0 %collective-permute-start.7 = (bf16[4,256,256]{2,1,0:T(8,128)(2,1)}, bf16[4,256,256]{2,1,0:T(8,128)(2,1)}, u32[]{:S(2)}, u32[]{:S(2)}) collective-permute-start(bf16[4,256,256]{2,1,0:T(8,128)(2,1)} %bitcast.25), channel_id=1, source_target_pairs={{2,0},{4,2},{6,4},{8,6},{10,8},{12,10},{14,12},{0,14},{3,1},{5,3},... | collective-permute-start | bytes 1572872 | tf_op jit(solution)/shard_map/ppermute | solution.py:338
  21.2 1.0 copy-start.3
  22.2 62.1 %collective-permute-start.9 = (bf16[2,2,256,256]{3,2,1,0:T(8,128)(2,1)}, bf16[2,2,256,256]{3,2,1,0:T(8,128)(2,1)}, u32[]{:S(2)}, u32[]{:S(2)}) collective-permute-start(bf16[2,2,256,256]{3,2,1,0:T(8,128)(2,1)} %get-tuple-element.65), channel_id=1, source_target_pairs={{0,1},{1,0},{2,3},{3,2},{4,5},{5,4},{6,7},{7,6},{8,9},{9,8},{10,11... | collective-permute-start | bytes 1572872 | tf_op jit(solution)/shard_map/ppermute | solution.py:387
  28.9 8.7 %copy-start.7 = (s32[4,64,2]{1,2,0:T(2,128)S(1)}, s32[4,64,2]{1,2,0:T(2,128)}, u32[]{:S(2)}) copy-start(s32[4,64,2]{1,2,0:T(2,128)} %param.28) | copy-start | bytes 6148
  28.9 8.8 %copy-start.10 = (s32[4,64]{1,0:T(4,128)S(1)}, s32[4,64]{1,0:T(4,128)}, u32[]{:S(2)}) copy-start(s32[4,64]{1,0:T(4,128)} %param.29) | copy-start | bytes 3076
  37.6 6.0 %collective-permute-start.3 = (bf16[256,256]{1,0:T(8,128)(2,1)S(1)}, bf16[256,256]{1,0:T(8,128)(2,1)S(1)}, u32[]{:S(2)}, u32[]{:S(2)}) collective-permute-start(bf16[256,256]{1,0:T(8,128)(2,1)S(1)} %pad_maximum_fusion.4), channel_id=1, source_target_pairs={{0,4},{2,6},{4,0},{6,2},{8,12},{10,14},{12,8},{14,10},{1,5},{3,7},... | collective-permute-start | bytes 393224 | tf_op jit(solution)/shard_map/ppermute | solution.py:404
  43.6 11.7 %copy-start.5 = (bf16[256,256]{1,0:T(8,128)(2,1)}, bf16[256,256]{1,0:T(8,128)(2,1)S(1)}, u32[]{:S(2)}) copy-start(bf16[256,256]{1,0:T(8,128)(2,1)S(1)} %collective-permute-done.3) | copy-start | bytes 393220
  43.6 14.4 %collective-permute-start.4 = (bf16[512,256]{1,0:T(8,128)(2,1)S(1)}, bf16[512,256]{1,0:T(8,128)(2,1)S(1)}, u32[]{:S(2)}, u32[]{:S(2)}) collective-permute-start(bf16[512,256]{1,0:T(8,128)(2,1)S(1)} %pad_maximum_fusion.3), channel_id=1, source_target_pairs={{0,8},{2,10},{4,12},{6,14},{8,0},{10,2},{12,4},{14,6},{1,9},{3,11}... | collective-permute-start | bytes 786440 | tf_op jit(solution)/shard_map/ppermute | solution.py:404
  59.0 40.9 %collective-permute-start.5 = (bf16[1024,256]{1,0:T(8,128)(2,1)S(1)}, bf16[1024,256]{1,0:T(8,128)(2,1)}, u32[]{:S(2)}, u32[]{:S(2)}) collective-permute-start(bf16[1024,256]{1,0:T(8,128)(2,1)S(1)} %pad_maximum_fusion.1.coeff), channel_id=1, source_target_pairs={{0,1},{1,0},{2,3},{3,2},{4,5},{5,4},{6,7},{7,6},{8,9},{9,8},{10,11... | collective-permute-start | bytes 1572872 | tf_op jit(solution)/shard_map/ppermute | solution.py:407
  59.1 25.2 %copy-start.4 = (bf16[2,4,256,256]{3,2,1,0:T(8,128)(2,1)S(1)}, bf16[2,4,256,256]{3,2,1,0:T(8,128)(2,1)}, u32[]{:S(2)}) copy-start(bf16[2,4,256,256]{3,2,1,0:T(8,128)(2,1)} %copy-done.3) | copy-start | bytes 3145732
  79.8 20.1 %collective-permute-start.1 = (bf16[2,4,256,256]{3,2,1,0:T(8,128)(2,1)}, bf16[2,4,256,256]{3,2,1,0:T(8,128)(2,1)S(1)}, u32[]{:S(2)}, u32[]{:S(2)}) collective-permute-start(bf16[2,4,256,256]{3,2,1,0:T(8,128)(2,1)} %get-tuple-element.62), channel_id=1, source_target_pairs={{0,1},{1,0},{2,3},{3,2},{4,5},{5,4},{6,7},{7,6},{8,9},{9,8},{10,11... | collective-permute-start | bytes 3145736 | tf_op jit(solution)/shard_map/ppermute | solution.py:427
  84.3 15.7 %collective-permute-start.8 = (bf16[2,2,256,256]{3,2,1,0:T(8,128)(2,1)}, bf16[2,2,256,256]{3,2,1,0:T(8,128)(2,1)}, u32[]{:S(2)}, u32[]{:S(2)}) collective-permute-start(bf16[2,2,256,256]{3,2,1,0:T(8,128)(2,1)} %bitcast.26), channel_id=1, source_target_pairs={{0,1},{1,0},{2,3},{3,2},{4,5},{5,4},{6,7},{7,6},{8,9},{9,8},{10,11... | collective-permute-start | bytes 1572872 | tf_op jit(solution)/shard_map/ppermute | solution.py:446
  86.4 27.8 %collective-permute-start.10 = (bf16[4,256,256]{2,1,0:T(8,128)(2,1)}, bf16[4,256,256]{2,1,0:T(8,128)(2,1)}, u32[]{:S(2)}, u32[]{:S(2)}) collective-permute-start(bf16[4,256,256]{2,1,0:T(8,128)(2,1)} %get-tuple-element.66), channel_id=1, source_target_pairs={{0,2},{2,4},{4,6},{6,8},{8,10},{10,12},{12,14},{14,0},{1,3},{3,5},... | collective-permute-start | bytes 1572872 | tf_op jit(solution)/shard_map/ppermute | solution.py:400
  86.4 27.8 %collective-permute-start.11 = (bf16[4,256,256]{2,1,0:T(8,128)(2,1)}, bf16[4,256,256]{2,1,0:T(8,128)(2,1)}, u32[]{:S(2)}, u32[]{:S(2)}) collective-permute-start(bf16[4,256,256]{2,1,0:T(8,128)(2,1)} %get-tuple-element.67), channel_id=1, source_target_pairs={{2,0},{4,2},{6,4},{8,6},{10,8},{12,10},{14,12},{0,14},{3,1},{5,3},... | collective-permute-start | bytes 1572872 | tf_op jit(solution)/shard_map/ppermute | solution.py:399
  114.2 1.6 %copy-start.1 = (f32[8,256,256]{2,1,0:T(8,128)S(1)}, f32[8,256,256]{2,1,0:T(8,128)}, u32[]{:S(2)}) copy-start(f32[8,256,256]{2,1,0:T(8,128)} %get-tuple-element.63.edge) | copy-start | bytes 6291460
